TPU v7x, 1024 devices: a whole 4x8x16 slice. The times are simulated.
1024 devices in a mesh: expert: 32 (over x, y), hidden: 32 (over z, core).
Axes of the slice: x: 4, y: 8, z: 16, core: 2. Of those that a mesh axis runs over, the one named last changes fastest.
Arguments:
- tokens: bfloat16 [4096, 4096], P('expert', 'hidden'), may hold values from -6 to 6
- upstream: bfloat16 [4096, 4096], P('expert', 'hidden'), may hold values from -6 to 6
- router: bfloat16 [4096, 32], replicated, may hold values from -0.09375 to 0.09375
- w_gate: bfloat16 [32, 4096, 4096], P('expert', None, 'hidden'), may hold values from -0.09375 to 0.09375
- w_up: bfloat16 [32, 4096, 4096], P('expert', None, 'hidden'), may hold values from -0.09375 to 0.09375
- w_down: bfloat16 [32, 4096, 4096], P('expert', 'hidden'), may hold values from -0.09375 to 0.09375
- chosen: int32 [32, 256], replicated, may hold values from 0 to 4095, as said below
Outputs:
- grad_tokens: bfloat16 [4096, 4096], P('expert', 'hidden')
Inputs may be any that keep to these rules, and one draw needn't show every extreme that they name: `chosen`: each row holds 256 distinct token indices. Of one expert's list at most 16 indices lie in one block of 128 consecutive tokens, and every expert has a block with exactly 16.
All inputs are finite; a program needn't handle non-finite values.
Results may differ from a plain program's by a relative error of at most 0.0056.
Values may be sent and summed in bfloat16 or wider, within the bound.
No kernel may reach another device: no remote copies, remote signals or barrier semaphores. Data moves between devices by JAX's collectives and lax.ppermute only.
A program may use at most 32 MiB of HBM per device.

v0:
```python
import jax
import jax.numpy as jnp
from jax import lax
from jax.experimental import pallas as pl
from jax.experimental.pallas import tpu as pltpu
from jax.sharding import PartitionSpec as P

F32 = jnp.float32
BF16 = jnp.bfloat16
SLOT = 16
LAST = (((1,), (1,)), ((), ()))
FIRST = (((0,), (0,)), ((), ()))
STEPS = (64, 16, 8, 4, 2, 1)
BASE = 13


def mm(a, b, dims=(((1,), (0,)), ((), ()))):
    return lax.dot_general(a, b, dims, preferred_element_type=F32)


def call(kernel, out, *args, flops=0, vmem=16, stream=False, scratch=()):
    spec = pl.BlockSpec(memory_space=pltpu.VMEM)
    moved = sum(a.size * a.dtype.itemsize for a in args) + sum(o.size * o.dtype.itemsize for o in out)
    return pl.pallas_call(
        kernel,
        out_shape=list(out),
        in_specs=[pl.BlockSpec(memory_space=pltpu.HBM) if stream else spec] * len(args),
        out_specs=[spec] * len(out),
        scratch_shapes=list(scratch),
        compiler_params=pltpu.CompilerParams(vmem_limit_bytes=vmem * 1024 * 1024),
        cost_estimate=pl.CostEstimate(flops=flops, bytes_accessed=moved, transcendentals=0),
    )(*args)


def shape(dims, dtype):
    return jax.ShapeDtypeStruct(dims, dtype)


def iota(dims, axis):
    return lax.broadcasted_iota(jnp.int32, dims, axis)


def route_kernel(chosen_hbm, tok_hbm, up_hbm, blocks_ref, sender_ref, packer_ref, chosen_ref, tok_ref, up_ref, sem):
    pairs = ((chosen_hbm, chosen_ref), (tok_hbm, tok_ref), (up_hbm, up_ref))
    loads = [pltpu.make_async_copy(a, b, sem.at[i]) for i, (a, b) in enumerate(pairs)]
    for load in loads:
        load.start()
    loads[0].wait()
    col = lax.axis_index("expert")
    experts, cap = chosen_ref.shape
    count = tok_ref.shape[0]
    slots = experts * SLOT
    token = iota((count, cap), 0) + col * count
    lane = iota((count, experts), 1)
    mask = jnp.zeros((count, experts), F32)
    for e in range(experts):
        hit = jnp.sum((chosen_ref[e : e + 1, :] == token).astype(F32), axis=1, keepdims=True)
        mask = jnp.where(lane == e, hit, mask)
    mask = mask.astype(BF16)
    earlier = (iota((count, count), 0) > iota((count, count), 1)).astype(F32).astype(BF16)
    rank = mm(earlier, mask).astype(BF16)
    spread = (iota((experts, slots), 1) // SLOT == iota((experts, slots), 0)).astype(F32).astype(BF16)
    place = (iota((count, slots), 1) % SLOT).astype(F32)
    sender = jnp.logical_and(mm(mask, spread) > 0.5, mm(rank, spread) == place).astype(F32).astype(BF16)
    sender_ref[...] = sender
    loads[1].wait()
    loads[2].wait()
    blocks_ref[...] = mm(sender, jnp.concatenate([tok_ref[...], up_ref[...]], axis=1), FIRST).astype(BF16)
    own = chosen_ref[pl.ds(col, 1), :] // count
    block = iota((slots, cap), 0) // SLOT
    held = jnp.sum((own == block).astype(F32), axis=1, keepdims=True)
    before = jnp.sum((own < block).astype(F32), axis=1, keepdims=True)
    place = (iota((slots, 1), 0) % SLOT).astype(F32)
    row = jnp.where(place < held, before + place, -1.0)
    packer_ref[...] = (row == iota((slots, cap), 1).astype(F32)).astype(F32).astype(BF16)


def scale_up(rows):
    top = jnp.max(jnp.max(jnp.abs(rows), axis=1, keepdims=True), axis=0, keepdims=True)
    power = jnp.zeros_like(top)
    factor = jnp.full_like(top, 2.0**BASE)
    for step in STEPS:
        small = top <= 2.0 ** (2 - step)
        top = jnp.where(small, top * 2.0**step, top)
        factor = jnp.where(small, factor * 2.0**step, factor)
        power = jnp.where(small, power + step, power)
    return rows * factor, power


def pack_kernel(arrived_ref, packer_ref, out_ref):
    cap = packer_ref.shape[1]
    half = arrived_ref.shape[1] // 2
    rows = mm(packer_ref[...], arrived_ref[...], FIRST)
    for part in range(2):
        lanes = slice(part * half, (part + 1) * half)
        scaled, power = scale_up(rows[:, lanes])
        out_ref[:cap, lanes] = scaled.astype(BF16)
        out_ref[cap:, lanes] = jnp.broadcast_to(power, (out_ref.shape[0] - cap, half)).astype(BF16)


def expert_kernel(x_ref, gate_ref, up_ref, down_ref, router_ref, sib_ref, grads_ref, slope_ref, row_ref):
    col = lax.axis_index("expert")
    hidden = lax.axis_index("hidden")
    core = hidden % 2
    chips = x_ref.shape[0] // 2
    rows = x_ref.shape[1]
    width = gate_ref.shape[1]
    picks = iota(router_ref.shape, 0) == col
    router = jnp.sum(jnp.where(picks, router_ref[...].astype(F32), 0.0), axis=0, keepdims=True)
    row_ref[...] = router

    def at(j):
        return slice(2 * j * width, 2 * (j + 1) * width)

    pre = jnp.zeros((rows, 2 * width), F32)
    back = jnp.zeros((rows, width), F32)
    logit = jnp.zeros((rows, width), F32)
    for j in range(chips):
        x = jnp.concatenate([x_ref[2 * j, :, :width], x_ref[2 * j + 1, :, :width]], axis=1)
        u = jnp.concatenate([x_ref[2 * j, :, width:], x_ref[2 * j + 1, :, width:]], axis=1)
        pre += mm(x, jnp.concatenate([gate_ref[at(j), :], up_ref[at(j), :]], axis=1))
        back += mm(u, down_ref[:, at(j)], LAST)
        logged = x.astype(F32) * router[:, at(j)]
        logit += logged[:, :width] + logged[:, width:]
    logit = jnp.sum(logit, axis=1, keepdims=True)
    weight = 1.0 / (1.0 + jnp.exp(-logit))
    gate_pre, up_pre = pre[:, :width], pre[:, width:]
    sig = 1.0 / (1.0 + jnp.exp(-gate_pre))
    act = (gate_pre * sig * up_pre).astype(BF16)
    score = jnp.sum(back * act.astype(F32), axis=1, keepdims=True)
    scaled = weight * back
    d_up = (scaled * gate_pre * sig).astype(BF16)
    d_gate = (scaled * up_pre * sig * (1.0 + gate_pre * (1.0 - sig))).astype(BF16)
    grads = jnp.concatenate([d_gate, d_up], axis=1)
    slope = score * (weight * (1.0 - weight))

    grads_ref[...] = grads
    slope_ref[...] = jnp.broadcast_to(slope, slope_ref.shape)
    core_terms(chips, 1 - core, grads, slope, gate_ref, up_ref, row_ref, sib_ref)


def core_terms(chips, core, grads, slope, gate_ref, up_ref, row_ref, out_ref):
    chip = lax.axis_index("hidden") // 2
    width = gate_ref.shape[1]
    part = chips // 4
    along = 1 + 2 * core
    for group, apart in enumerate((0, 4 - along, 2, along)):

        def features(r):
            target = 4 * r + (chip + apart) % 4
            return pl.ds(pl.multiple_of((2 * target + core) * width, width), width)

        for first in range(0, part, 2):
            some = range(first, min(first + 2, part))
            side = [jnp.concatenate([gate_ref[features(r), :], up_ref[features(r), :]], axis=1) for r in some]
            terms = mm(grads, jnp.concatenate(side, axis=0), LAST)
            for i, r in enumerate(some):
                out = terms[:, i * width : (i + 1) * width] + slope * row_ref[:, features(r)]
                out_ref[group * part + r] = out.astype(out_ref.dtype)


def terms_kernel(grads_ref, slope_ref, row_ref, gate_ref, up_ref, own_ref):
    core = lax.axis_index("hidden") % 2
    chips = gate_ref.shape[0] // (2 * gate_ref.shape[1])
    core_terms(chips, core, grads_ref[...], slope_ref[:, :1], gate_ref, up_ref, row_ref, own_ref)


def body(tokens, upstream, router, w_gate, w_up, w_down, chosen):
    experts = lax.axis_size("expert")
    devices = lax.axis_size("hidden")
    chips = devices // 2
    count, width = tokens.shape
    cap = chosen.shape[1]
    slots = experts * SLOT

    blocks, sender, packer = call(
        route_kernel,
        [shape((slots, 2 * width), BF16), shape((count, slots), BF16), shape((slots, cap), BF16)],
        chosen, tokens, upstream,
        stream=True,
        scratch=[
            pltpu.VMEM(chosen.shape, jnp.int32),
            pltpu.VMEM(tokens.shape, BF16),
            pltpu.VMEM(upstream.shape, BF16),
            pltpu.SemaphoreType.DMA((3,)),
        ],
    )
    arrived = lax.all_to_all(blocks.reshape(experts, SLOT, 2 * width), "expert", 0, 0, tiled=True)
    (rows,) = call(pack_kernel, [shape((cap + 16, 2 * width), BF16)], arrived.reshape(slots, 2 * width), packer)
    full = lax.all_gather(rows.astype(jnp.float16), "hidden", axis=0)
    undo = jnp.exp2(-(full[:, cap : cap + 1, :].astype(F32) + BASE))
    picked = (full[:, :cap, :].astype(F32) * undo).astype(BF16)

    gate, up = w_gate[0], w_up[0]
    sibling, grads, slope, row = call(
        expert_kernel,
        [
            shape((chips, cap, width), BF16), shape((cap, 2 * width), BF16), shape((cap, width), F32),
            shape((1, devices * width), F32),
        ],
        picked, gate, up, w_down[0], router.T,
        flops=8 * cap * devices * width * width,
        vmem=24,
    )
    arrived = lax.ppermute(sibling, "hidden", [(i, i ^ 1) for i in range(devices)])
    (own,) = call(
        terms_kernel,
        [shape((chips, cap, width), F32)],
        grads, slope, row, gate, up,
        flops=8 * cap * devices * width * width,
        vmem=24,
    )

    part = chips // 4

    def both(group):
        at = slice(group * part, (group + 1) * part)
        return own[at] + arrived[at].astype(F32)

    def shift(v, hops):
        to = [(i, (i + 2 * hops * (1 - 2 * (i % 2))) % devices) for i in range(devices)]
        return lax.ppermute(v.astype(BF16), "hidden", to).astype(F32)

    passed = shift(both(2), 1)
    near = (both(0) + shift(both(1), -1) + shift(both(3) + passed, 1)).astype(BF16)
    groups = [[c + 2 * q + 8 * r for r in range(part)] for q in range(4) for c in range(2)]
    parts = lax.all_to_all(near, "hidden", 0, 0, tiled=True, axis_index_groups=groups)
    slot_grad = jnp.sum(parts.astype(F32), axis=0).astype(BF16)
    outgoing = mm(packer, slot_grad).astype(BF16)
    arrived = lax.all_to_all(outgoing.reshape(experts, SLOT, width), "expert", 0, 0, tiled=True)
    return mm(sender, arrived.reshape(slots, width)).astype(BF16)


def solution(mesh):
    in_specs = (
        P("expert", "hidden"),
        P("expert", "hidden"),
        P(),
        P("expert", None, "hidden"),
        P("expert", None, "hidden"),
        P("expert", "hidden", None),
        P(),
    )
    out_specs = P("expert", "hidden")
    return jax.shard_map(body, mesh=mesh, in_specs=in_specs, out_specs=out_specs, check_vma=False)
```

profile of v0, /device:TPU:8, one launch (start us, length us, event | category | flops | bytes accessed | tf_op | source)
XLA Modules:
  0.0 148.9 jit_solution(4762635099562671339)
XLA Ops:
  0.0 0.0 copy-start.4
  0.0 0.8 copy-done.4
  0.8 0.0 copy-start.5
  0.8 0.8 copy-done.5
  1.5 0.0 copy-start.6
  1.5 0.8 copy-done.6
  2.3 1.3 shard_map.73
  3.6 26.8 %all_to_all.15 = bf16[32,16,256]{2,1,0:T(8,128)(2,1)S(1)} all-to-all(bf16[32,16,256]{2,1,0:T(8,128)(2,1)S(1)} %bitcast.22), channel_id=1, replica_groups=mesh['expert'=32,'hidden'=32] {'expert'}, dimensions={0} | all-to-all | bytes 524288 | tf_op jit(solution)/shard_map/all_to_all | solution.py:188
  30.4 0.4 shard_map.74
  30.9 52.4 %all-gather.2 = f16[8704,256]{1,0:T(8,128)(2,1)S(1)} all-gather(f16[272,256]{1,0:T(8,128)(2,1)S(1)} %convert_element_type.53), channel_id=2, replica_groups=mesh['expert'=32,'hidden'=32] {'hidden'}, dimensions={0}, use_global_device_ids=true | all-gather | bytes 4595712 | tf_op jit(solution)/shard_map/all_gather | solution.py:190
  83.3 0.1 fusion.10
  83.4 0.0 copy-start
  83.4 0.0 copy-start.1
  83.4 0.0 copy-start.2
  83.4 0.0 copy-start.3
  83.4 1.0 multiply_convert_fusion.x_ref
  84.5 0.1 copy-done
  84.6 0.3 copy-done.1
  84.9 0.3 copy-done.2
  85.2 0.0 copy-done.3
  85.3 1.7 %shard_map.75 = (bf16[16,256,128]{2,1,0:T(8,128)(2,1)S(1)}, bf16[256,256]{1,0:T(8,128)(2,1)S(1)}, f32[256,128]{1,0:T(8,128)S(1)}, f32[1,4096]{1,0:T(1,128)S(1)}) custom-call(bf16[32,256,256]{2,1,0:T(8,128)(2,1)S(1)} %multiply_convert_fusion.x_ref, bf16[4096,128]{1,0:T(8,128)(2,1)S(1)} %bitcast.16, bf16[4096,128]{1,0:T(8,128)(2,1)S(1)} %bitcast.18, ...), custom_call_target="tpu_custom_call" | custom-call | flops 1073741824 | bytes 8929280 | tf_op jit(solution)/shard_map/pallas_call | solution.py:24
  87.0 2.3 %collective-permute-start = (bf16[16,256,128]{2,1,0:T(8,128)(2,1)S(1)}, bf16[16,256,128]{2,1,0:T(8,128)(2,1)S(1)}, u32[]{:S(2)}, u32[]{:S(2)}) collective-permute-start(bf16[16,256,128]{2,1,0:T(8,128)(2,1)S(1)} %get-tuple-element.18), channel_id=1, source_target_pairs={{0,1},{1,0},{2,3},{3,2},{4,5},{5,4},{6,7},{7,6},{8,9},{9,8},{10,11... | collective-permute-start | bytes 3145736 | tf_op jit(solution)/shard_map/ppermute | solution.py:205
  89.3 0.5 shard_map.76
  89.8 1.8 %collective-permute-done = bf16[16,256,128]{2,1,0:T(8,128)(2,1)S(1)} collective-permute-done((bf16[16,256,128]{2,1,0:T(8,128)(2,1)S(1)}, bf16[16,256,128]{2,1,0:T(8,128)(2,1)S(1)}, u32[]{:S(2)}, u32[]{:S(2)}) %collective-permute-start) | collective-permute-done | bytes 1048608 | tf_op jit(solution)/shard_map/ppermute | solution.py:205
  91.5 0.1 fusion.3
  91.6 4.5 %collective-permute-start.2 = (bf16[4,256,128]{2,1,0:T(8,128)(2,1)S(1)}, bf16[4,256,128]{2,1,0:T(8,128)(2,1)S(1)}, u32[]{:S(2)}, u32[]{:S(2)}) collective-permute-start(bf16[4,256,128]{2,1,0:T(8,128)(2,1)S(1)} %get-tuple-element.20), channel_id=1, source_target_pairs={{0,2},{1,31},{2,4},{3,1},{4,6},{5,3},{6,8},{7,5},{8,10},{9,7},{10,... | collective-permute-start | bytes 786440 | tf_op jit(solution)/shard_map/ppermute | solution.py:222
  96.2 2.5 %collective-permute-start.1 = (bf16[4,256,128]{2,1,0:T(8,128)(2,1)S(1)}, bf16[4,256,128]{2,1,0:T(8,128)(2,1)S(1)}, u32[]{:S(2)}, u32[]{:S(2)}) collective-permute-start(bf16[4,256,128]{2,1,0:T(8,128)(2,1)S(1)} %get-tuple-element.19), channel_id=1, source_target_pairs={{0,30},{1,3},{2,0},{3,5},{4,2},{5,7},{6,4},{7,9},{8,6},{9,11},{10,... | collective-permute-start | bytes 786440 | tf_op jit(solution)/shard_map/ppermute | solution.py:222
  98.7 2.8 %collective-permute-done.2 = bf16[4,256,128]{2,1,0:T(8,128)(2,1)S(1)} collective-permute-done((bf16[4,256,128]{2,1,0:T(8,128)(2,1)S(1)}, bf16[4,256,128]{2,1,0:T(8,128)(2,1)S(1)}, u32[]{:S(2)}, u32[]{:S(2)}) %collective-permute-start.2) | collective-permute-done | bytes 262176 | tf_op jit(solution)/shard_map/ppermute | solution.py:222
  101.5 0.1 fusion.2
  101.6 4.4 %collective-permute-start.3 = (bf16[4,256,128]{2,1,0:T(8,128)(2,1)S(1)}, bf16[4,256,128]{2,1,0:T(8,128)(2,1)S(1)}, u32[]{:S(2)}, u32[]{:S(2)}) collective-permute-start(bf16[4,256,128]{2,1,0:T(8,128)(2,1)S(1)} %fusion.2), channel_id=1, source_target_pairs={{0,2},{1,31},{2,4},{3,1},{4,6},{5,3},{6,8},{7,5},{8,10},{9,7},{10,... | collective-permute-start | bytes 786440 | tf_op jit(solution)/shard_map/ppermute | solution.py:222
  106.0 0.0 collective-permute-done.1
  106.0 5.1 %collective-permute-done.3 = bf16[4,256,128]{2,1,0:T(8,128)(2,1)S(1)} collective-permute-done((bf16[4,256,128]{2,1,0:T(8,128)(2,1)S(1)}, bf16[4,256,128]{2,1,0:T(8,128)(2,1)S(1)}, u32[]{:S(2)}, u32[]{:S(2)}) %collective-permute-start.3) | collective-permute-done | bytes 262176 | tf_op jit(solution)/shard_map/ppermute | solution.py:222
  111.0 0.1 fusion.6
  111.2 22.6 %all_to_all.16 = bf16[4,256,128]{2,1,0:T(8,128)(2,1)S(1)} all-to-all(bf16[4,256,128]{2,1,0:T(8,128)(2,1)S(1)} %fusion.6), channel_id=1, replica_groups={{0,8,16,24},{1,9,17,25},{2,10,18,26},{3,11,19,27},{4,12,20,28},{5,13,21..., dimensions={0} | all-to-all | bytes 524288 | tf_op jit(solution)/shard_map/all_to_all | solution.py:227
  133.8 0.2 convolution_convert_fusion
  134.0 14.0 %all_to_all.17 = bf16[32,16,128]{2,1,0:T(8,128)(2,1)S(1)} all-to-all(bf16[32,16,128]{2,1,0:T(8,128)(2,1)S(1)} %bitcast.26), channel_id=1, replica_groups=mesh['expert'=32,'hidden'=32] {'expert'}, dimensions={0} | all-to-all | bytes 262144 | tf_op jit(solution)/shard_map/all_to_all | solution.py:230
  148.1 0.8 convolution_convert_fusion.1
  (3 shorter events, 0.1 us)
Async XLA Ops:
  0.0 0.8 copy-start.4
  0.8 0.8 copy-start.5
  1.5 0.8 copy-start.6
  83.4 1.2 copy-start
  83.4 1.5 %copy-start.1 = (bf16[1,4096,128]{2,1,0:T(8,128)(2,1)S(1)}, bf16[1,4096,128]{2,1,0:T(8,128)(2,1)}, u32[]{:S(2)}) copy-start(bf16[1,4096,128]{2,1,0:T(8,128)(2,1)} %param.11) | copy-start | bytes 3145732
  83.4 1.8 %copy-start.2 = (bf16[1,128,4096]{2,1,0:T(8,128)(2,1)S(1)}, bf16[1,128,4096]{2,1,0:T(8,128)(2,1)}, u32[]{:S(2)}) copy-start(bf16[1,128,4096]{2,1,0:T(8,128)(2,1)} %param.12) | copy-start | bytes 3145732
  83.4 1.9 %copy-start.3 = (bf16[4096,32]{0,1:T(8,128)(2,1)S(1)}, bf16[4096,32]{0,1:T(8,128)(2,1)}, u32[]{:S(2)}) copy-start(bf16[4096,32]{0,1:T(8,128)(2,1)} %param.9) | copy-start | bytes 786436
  87.0 4.6 %collective-permute-start = (bf16[16,256,128]{2,1,0:T(8,128)(2,1)S(1)}, bf16[16,256,128]{2,1,0:T(8,128)(2,1)S(1)}, u32[]{:S(2)}, u32[]{:S(2)}) collective-permute-start(bf16[16,256,128]{2,1,0:T(8,128)(2,1)S(1)} %get-tuple-element.18), channel_id=1, source_target_pairs={{0,1},{1,0},{2,3},{3,2},{4,5},{5,4},{6,7},{7,6},{8,9},{9,8},{10,11... | collective-permute-start | bytes 3145736 | tf_op jit(solution)/shard_map/ppermute | solution.py:205
  91.6 9.8 %collective-permute-start.2 = (bf16[4,256,128]{2,1,0:T(8,128)(2,1)S(1)}, bf16[4,256,128]{2,1,0:T(8,128)(2,1)S(1)}, u32[]{:S(2)}, u32[]{:S(2)}) collective-permute-start(bf16[4,256,128]{2,1,0:T(8,128)(2,1)S(1)} %get-tuple-element.20), channel_id=1, source_target_pairs={{0,2},{1,31},{2,4},{3,1},{4,6},{5,3},{6,8},{7,5},{8,10},{9,7},{10,... | collective-permute-start | bytes 786440 | tf_op jit(solution)/shard_map/ppermute | solution.py:222
  96.2 9.8 %collective-permute-start.1 = (bf16[4,256,128]{2,1,0:T(8,128)(2,1)S(1)}, bf16[4,256,128]{2,1,0:T(8,128)(2,1)S(1)}, u32[]{:S(2)}, u32[]{:S(2)}) collective-permute-start(bf16[4,256,128]{2,1,0:T(8,128)(2,1)S(1)} %get-tuple-element.19), channel_id=1, source_target_pairs={{0,30},{1,3},{2,0},{3,5},{4,2},{5,7},{6,4},{7,9},{8,6},{9,11},{10,... | collective-permute-start | bytes 786440 | tf_op jit(solution)/shard_map/ppermute | solution.py:222
  101.6 9.5 %collective-permute-start.3 = (bf16[4,256,128]{2,1,0:T(8,128)(2,1)S(1)}, bf16[4,256,128]{2,1,0:T(8,128)(2,1)S(1)}, u32[]{:S(2)}, u32[]{:S(2)}) collective-permute-start(bf16[4,256,128]{2,1,0:T(8,128)(2,1)S(1)} %fusion.2), channel_id=1, source_target_pairs={{0,2},{1,31},{2,4},{3,1},{4,6},{5,3},{6,8},{7,5},{8,10},{9,7},{10,... | collective-permute-start | bytes 786440 | tf_op jit(solution)/shard_map/ppermute | solution.py:222
where the time goes:
time: 149 us
  blocking collectives  116 us (78%)
  starting transfers between devices  13.7 us (9%)
  waiting for transfers between devices  9.6 us (6%)
  Pallas kernels  3.92 us (3%)
  local copies, waits for them, and re-layouts  3.11 us (2%)
    all_gather x1, blocking collectives, body(): full = lax.all_gather(rows.astype(jnp.float16), 'hidden', axis=0)  52.4 us
    all_to_all x1, blocking collectives, body(): lax.all_to_all(blocks.reshape(experts, SLOT, 2 * width), 'expert', 0, 0,...  26.8 us
    all_to_all x1, blocking collectives, body(): lax.all_to_all(near, 'hidden', 0, 0, tiled=True, axis_index_groups=groups)  22.6 us
    all_to_all x1, blocking collectives, body(): lax.all_to_all(outgoing.reshape(experts, SLOT, width), 'expert', 0, 0, ti...  14 us
    ppermute x3, starting transfers between devices, shift(): return lax.ppermute(v.astype(BF16), 'hidden', to).astype(F32)  11.4 us
    ppermute x3, waiting for transfers between devices, shift(): return lax.ppermute(v.astype(BF16), 'hidden', to).astype(F32)  7.83 us
    pallas_call x4, Pallas kernels, call(): pl.pallas_call(kernel, out_shape=list(out), in_specs=[pl.BlockSpec(memory...  3.92 us
    unnamed x15, local copies, waits for them, and re-layouts  3.11 us
  transfers between devices with their start and end apart: 4, of which 3 were waited for; matrix products, arithmetic and copies ran while one was open for 0% of the time, Pallas kernels for 0%

commit v1 on v0

--- a/solution.py
+++ b/solution.py
@@ -222,10 +222,16 @@
         return lax.ppermute(v.astype(BF16), "hidden", to).astype(F32)
 
     passed = shift(both(2), 1)
-    near = (both(0) + shift(both(1), -1) + shift(both(3) + passed, 1)).astype(BF16)
-    groups = [[c + 2 * q + 8 * r for r in range(part)] for q in range(4) for c in range(2)]
-    parts = lax.all_to_all(near, "hidden", 0, 0, tiled=True, axis_index_groups=groups)
-    slot_grad = jnp.sum(parts.astype(F32), axis=0).astype(BF16)
+    near = both(0) + shift(both(1), -1) + shift(both(3) + passed, 1)
+
+    along = 1 + 2 * (lax.axis_index("hidden") % 2)
+
+    def piece(apart):
+        return lax.dynamic_index_in_dim(near, (lax.axis_index("hidden") // 8 + apart) % part, 0, keepdims=False)
+
+    passed = shift(piece(2), 4)
+    total = piece(0) + shift(piece(4 - along), -4) + shift(piece(along) + passed, 4)
+    slot_grad = total.astype(BF16)
     outgoing = mm(packer, slot_grad).astype(BF16)
     arrived = lax.all_to_all(outgoing.reshape(experts, SLOT, width), "expert", 0, 0, tiled=True)
     return mm(sender, arrived.reshape(slots, width)).astype(BF16)

time: 149 us -> 153 us (1.027)
  blocking collectives: 116 us -> 93.7 us
  waiting for transfers between devices: 9.6 us -> 21.5 us
  starting transfers between devices: 13.7 us -> 25.4 us
  other arithmetic: 1.47 us -> 3.24 us
    all_to_all x1 -> x0, blocking collectives: 22.6 us -> none  [body(): lax.all_to_all(near, 'hidden', 0, 0, tiled=True, axis_index_groups=groups)]
    ppermute x3 -> x6, waiting for transfers between devices: 7.83 us -> 19.7 us  [shift(): return lax.ppermute(v.astype(BF16), 'hidden', to).astype(F32)]
    ppermute x3 -> x6, starting transfers between devices: 11.4 us -> 23.1 us  [shift(): return lax.ppermute(v.astype(BF16), 'hidden', to).astype(F32)]
    unnamed x15 -> x17, local copies, waits for them, and re-layouts: 3.11 us -> 3.11 us
  transfers between devices with their start and end apart: 4 -> 7, of which waited for: 3 -> 5; matrix products, arithmetic and copies ran while one was open for 0% -> 0% of each run, Pallas kernels for 0% -> 0%
where the time goes in v1:
time: 153 us; the launch traced here: 152 us
  blocking collectives  93.7 us (61%)
  starting transfers between devices  25.4 us (17%)
  waiting for transfers between devices  21.5 us (14%)
  Pallas kernels  3.92 us (3%)
  other arithmetic  3.24 us (2%)
  local copies, waits for them, and re-layouts  3.14 us (2%)
    all_gather x1, blocking collectives, body(): full = lax.all_gather(rows.astype(jnp.float16), 'hidden', axis=0)  52.4 us
    all_to_all x1, blocking collectives, body(): lax.all_to_all(blocks.reshape(experts, SLOT, 2 * width), 'expert', 0, 0,...  26.8 us
    ppermute x6, starting transfers between devices, shift(): return lax.ppermute(v.astype(BF16), 'hidden', to).astype(F32)  23.1 us
    ppermute x6, waiting for transfers between devices, shift(): return lax.ppermute(v.astype(BF16), 'hidden', to).astype(F32)  19.7 us
    all_to_all x1, blocking collectives, body(): lax.all_to_all(outgoing.reshape(experts, SLOT, width), 'expert', 0, 0, ti...  14.5 us
    pallas_call x4, Pallas kernels, call(): pl.pallas_call(kernel, out_shape=list(out), in_specs=[pl.BlockSpec(memory...  3.92 us
    unnamed x17, local copies, waits for them, and re-layouts  3.11 us
  transfers between devices with their start and end apart: 7, of which 5 were waited for; matrix products, arithmetic and copies ran while one was open for 0% of the time, Pallas kernels for 0%

profile of v1, /device:TPU:8, one launch (start us, length us, event | category | flops | bytes accessed | tf_op | source)
XLA Modules:
  0.0 152.2 jit_solution(16624849327695511338)
XLA Ops:
  0.0 0.0 copy-start.4
  0.0 0.8 copy-done.4
  0.8 0.0 copy-start.5
  0.8 0.8 copy-done.5
  1.5 0.0 copy-start.6
  1.5 0.8 copy-done.6
  2.3 1.3 shard_map.73
  3.6 26.8 %all_to_all.10 = bf16[32,16,256]{2,1,0:T(8,128)(2,1)S(1)} all-to-all(bf16[32,16,256]{2,1,0:T(8,128)(2,1)S(1)} %bitcast.36), channel_id=1, replica_groups=mesh['expert'=32,'hidden'=32] {'expert'}, dimensions={0} | all-to-all | bytes 524288 | tf_op jit(solution)/shard_map/all_to_all | solution.py:188
  30.4 0.4 shard_map.74
  30.9 52.4 %all-gather.2 = f16[8704,256]{1,0:T(8,128)(2,1)S(1)} all-gather(f16[272,256]{1,0:T(8,128)(2,1)S(1)} %convert_element_type.75), channel_id=2, replica_groups=mesh['expert'=32,'hidden'=32] {'hidden'}, dimensions={0}, use_global_device_ids=true | all-gather | bytes 4595712 | tf_op jit(solution)/shard_map/all_gather | solution.py:190
  83.3 0.1 fusion.15
  83.4 0.0 copy-start
  83.4 0.0 copy-start.1
  83.4 0.0 copy-start.2
  83.4 0.0 copy-start.3
  83.4 1.0 multiply_convert_fusion.x_ref
  84.5 0.1 copy-done
  84.6 0.3 copy-done.1
  84.9 0.3 copy-done.2
  85.2 0.0 copy-done.3
  85.3 1.7 %shard_map.75 = (bf16[16,256,128]{2,1,0:T(8,128)(2,1)S(1)}, bf16[256,256]{1,0:T(8,128)(2,1)S(1)}, f32[256,128]{1,0:T(8,128)S(1)}, f32[1,4096]{1,0:T(1,128)S(1)}) custom-call(bf16[32,256,256]{2,1,0:T(8,128)(2,1)S(1)} %multiply_convert_fusion.x_ref, bf16[4096,128]{1,0:T(8,128)(2,1)S(1)} %bitcast.30, bf16[4096,128]{1,0:T(8,128)(2,1)S(1)} %bitcast.32, ...), custom_call_target="tpu_custom_call" | custom-call | flops 1073741824 | bytes 8929280 | tf_op jit(solution)/shard_map/pallas_call | solution.py:24
  87.0 2.3 %collective-permute-start = (bf16[16,256,128]{2,1,0:T(8,128)(2,1)S(1)}, bf16[16,256,128]{2,1,0:T(8,128)(2,1)S(1)}, u32[]{:S(2)}, u32[]{:S(2)}) collective-permute-start(bf16[16,256,128]{2,1,0:T(8,128)(2,1)S(1)} %get-tuple-element.18), channel_id=1, source_target_pairs={{0,1},{1,0},{2,3},{3,2},{4,5},{5,4},{6,7},{7,6},{8,9},{9,8},{10,11... | collective-permute-start | bytes 3145736 | tf_op jit(solution)/shard_map/ppermute | solution.py:205
  89.3 0.5 shard_map.76
  89.8 1.8 %collective-permute-done = bf16[16,256,128]{2,1,0:T(8,128)(2,1)S(1)} collective-permute-done((bf16[16,256,128]{2,1,0:T(8,128)(2,1)S(1)}, bf16[16,256,128]{2,1,0:T(8,128)(2,1)S(1)}, u32[]{:S(2)}, u32[]{:S(2)}) %collective-permute-start) | collective-permute-done | bytes 1048608 | tf_op jit(solution)/shard_map/ppermute | solution.py:205
  91.5 0.0 copy-start.7
  91.5 1.0 fusion.3
  92.5 4.5 %collective-permute-start.2 = (bf16[4,256,128]{2,1,0:T(8,128)(2,1)S(1)}, bf16[4,256,128]{2,1,0:T(8,128)(2,1)S(1)}, u32[]{:S(2)}, u32[]{:S(2)}) collective-permute-start(bf16[4,256,128]{2,1,0:T(8,128)(2,1)S(1)} %get-tuple-element.20), channel_id=1, source_target_pairs={{0,2},{1,31},{2,4},{3,1},{4,6},{5,3},{6,8},{7,5},{8,10},{9,7},{10,... | collective-permute-start | bytes 786440 | tf_op jit(solution)/shard_map/ppermute | solution.py:222
  97.0 2.5 %collective-permute-start.1 = (bf16[4,256,128]{2,1,0:T(8,128)(2,1)}, bf16[4,256,128]{2,1,0:T(8,128)(2,1)S(1)}, u32[]{:S(2)}, u32[]{:S(2)}) collective-permute-start(bf16[4,256,128]{2,1,0:T(8,128)(2,1)} %get-tuple-element.19), channel_id=1, source_target_pairs={{0,30},{1,3},{2,0},{3,5},{4,2},{5,7},{6,4},{7,9},{8,6},{9,11},{10,... | collective-permute-start | bytes 786440 | tf_op jit(solution)/shard_map/ppermute | solution.py:222
  99.6 2.5 %collective-permute-done.2 = bf16[4,256,128]{2,1,0:T(8,128)(2,1)S(1)} collective-permute-done((bf16[4,256,128]{2,1,0:T(8,128)(2,1)S(1)}, bf16[4,256,128]{2,1,0:T(8,128)(2,1)S(1)}, u32[]{:S(2)}, u32[]{:S(2)}) %collective-permute-start.2) | collective-permute-done | bytes 262176 | tf_op jit(solution)/shard_map/ppermute | solution.py:222
  102.1 0.0 copy-done.7
  102.1 0.1 fusion.2
  102.2 4.4 %collective-permute-start.3 = (bf16[4,256,128]{2,1,0:T(8,128)(2,1)S(1)}, bf16[4,256,128]{2,1,0:T(8,128)(2,1)S(1)}, u32[]{:S(2)}, u32[]{:S(2)}) collective-permute-start(bf16[4,256,128]{2,1,0:T(8,128)(2,1)S(1)} %fusion.2), channel_id=1, source_target_pairs={{0,2},{1,31},{2,4},{3,1},{4,6},{5,3},{6,8},{7,5},{8,10},{9,7},{10,... | collective-permute-start | bytes 786440 | tf_op jit(solution)/shard_map/ppermute | solution.py:222
  106.6 0.0 collective-permute-done.1
  106.7 5.0 %collective-permute-done.3 = bf16[4,256,128]{2,1,0:T(8,128)(2,1)S(1)} collective-permute-done((bf16[4,256,128]{2,1,0:T(8,128)(2,1)S(1)}, bf16[4,256,128]{2,1,0:T(8,128)(2,1)S(1)}, u32[]{:S(2)}, u32[]{:S(2)}) %collective-permute-start.3) | collective-permute-done | bytes 262176 | tf_op jit(solution)/shard_map/ppermute | solution.py:222
  111.7 1.1 fusion.5
  112.8 3.6 %collective-permute-start.5 = (bf16[256,128]{1,0:T(8,128)(2,1)S(1)}, bf16[256,128]{1,0:T(8,128)(2,1)S(1)}, u32[]{:S(2)}, u32[]{:S(2)}) collective-permute-start(bf16[256,128]{1,0:T(8,128)(2,1)S(1)} %get-tuple-element.22), channel_id=1, source_target_pairs={{0,8},{1,25},{2,10},{3,27},{4,12},{5,29},{6,14},{7,31},{8,16},{9,1... | collective-permute-start | bytes 196616 | tf_op jit(solution)/shard_map/ppermute | solution.py:222
  116.4 6.2 %collective-permute-start.4 = (bf16[256,128]{1,0:T(8,128)(2,1)S(1)}, bf16[256,128]{1,0:T(8,128)(2,1)S(1)}, u32[]{:S(2)}, u32[]{:S(2)}) collective-permute-start(bf16[256,128]{1,0:T(8,128)(2,1)S(1)} %get-tuple-element.21), channel_id=1, source_target_pairs={{0,24},{1,9},{2,26},{3,11},{4,28},{5,13},{6,30},{7,15},{8,0},{9,17... | collective-permute-start | bytes 196616 | tf_op jit(solution)/shard_map/ppermute | solution.py:222
  122.5 3.7 %collective-permute-done.5 = bf16[256,128]{1,0:T(8,128)(2,1)S(1)} collective-permute-done((bf16[256,128]{1,0:T(8,128)(2,1)S(1)}, bf16[256,128]{1,0:T(8,128)(2,1)S(1)}, u32[]{:S(2)}, u32[]{:S(2)}) %collective-permute-start.5) | collective-permute-done | bytes 65568 | tf_op jit(solution)/shard_map/ppermute | solution.py:222
  126.2 1.9 %collective-permute-start.6 = (bf16[256,128]{1,0:T(8,128)(2,1)S(1)}, bf16[256,128]{1,0:T(8,128)(2,1)S(1)}, u32[]{:S(2)}, u32[]{:S(2)}) collective-permute-start(bf16[256,128]{1,0:T(8,128)(2,1)S(1)} %fusion.6), channel_id=1, source_target_pairs={{0,8},{1,25},{2,10},{3,27},{4,12},{5,29},{6,14},{7,31},{8,16},{9,1... | collective-permute-start | bytes 196616 | tf_op jit(solution)/shard_map/ppermute | solution.py:222
  128.2 0.0 collective-permute-done.4
  128.2 8.5 %collective-permute-done.6 = bf16[256,128]{1,0:T(8,128)(2,1)S(1)} collective-permute-done((bf16[256,128]{1,0:T(8,128)(2,1)S(1)}, bf16[256,128]{1,0:T(8,128)(2,1)S(1)}, u32[]{:S(2)}, u32[]{:S(2)}) %collective-permute-start.6) | collective-permute-done | bytes 65568 | tf_op jit(solution)/shard_map/ppermute | solution.py:222
  136.7 0.2 convolution_convert_fusion
  136.9 14.5 %all_to_all.11 = bf16[32,16,128]{2,1,0:T(8,128)(2,1)S(1)} all-to-all(bf16[32,16,128]{2,1,0:T(8,128)(2,1)S(1)} %bitcast.41), channel_id=1, replica_groups=mesh['expert'=32,'hidden'=32] {'expert'}, dimensions={0} | all-to-all | bytes 262144 | tf_op jit(solution)/shard_map/all_to_all | solution.py:236
  151.4 0.8 convolution_convert_fusion.1
  (4 shorter events, 0.1 us)
Async XLA Ops:
  0.0 0.8 copy-start.4
  0.8 0.8 copy-start.5
  1.5 0.8 copy-start.6
  83.4 1.2 copy-start
  83.4 1.5 %copy-start.1 = (bf16[1,4096,128]{2,1,0:T(8,128)(2,1)S(1)}, bf16[1,4096,128]{2,1,0:T(8,128)(2,1)}, u32[]{:S(2)}) copy-start(bf16[1,4096,128]{2,1,0:T(8,128)(2,1)} %param.11) | copy-start | bytes 3145732
  83.4 1.8 %copy-start.2 = (bf16[1,128,4096]{2,1,0:T(8,128)(2,1)S(1)}, bf16[1,128,4096]{2,1,0:T(8,128)(2,1)}, u32[]{:S(2)}) copy-start(bf16[1,128,4096]{2,1,0:T(8,128)(2,1)} %param.12) | copy-start | bytes 3145732
  83.4 1.9 %copy-start.3 = (bf16[4096,32]{0,1:T(8,128)(2,1)S(1)}, bf16[4096,32]{0,1:T(8,128)(2,1)}, u32[]{:S(2)}) copy-start(bf16[4096,32]{0,1:T(8,128)(2,1)} %param.9) | copy-start | bytes 786436
  87.0 4.6 %collective-permute-start = (bf16[16,256,128]{2,1,0:T(8,128)(2,1)S(1)}, bf16[16,256,128]{2,1,0:T(8,128)(2,1)S(1)}, u32[]{:S(2)}, u32[]{:S(2)}) collective-permute-start(bf16[16,256,128]{2,1,0:T(8,128)(2,1)S(1)} %get-tuple-element.18), channel_id=1, source_target_pairs={{0,1},{1,0},{2,3},{3,2},{4,5},{5,4},{6,7},{7,6},{8,9},{9,8},{10,11... | collective-permute-start | bytes 3145736 | tf_op jit(solution)/shard_map/ppermute | solution.py:205
  91.5 10.6 %copy-start.7 = (bf16[16,256,128]{2,1,0:T(8,128)(2,1)}, bf16[16,256,128]{2,1,0:T(8,128)(2,1)S(1)}, u32[]{:S(2)}) copy-start(bf16[16,256,128]{2,1,0:T(8,128)(2,1)S(1)} %collective-permute-done) | copy-start | bytes 3145732
  92.5 9.6 %collective-permute-start.2 = (bf16[4,256,128]{2,1,0:T(8,128)(2,1)S(1)}, bf16[4,256,128]{2,1,0:T(8,128)(2,1)S(1)}, u32[]{:S(2)}, u32[]{:S(2)}) collective-permute-start(bf16[4,256,128]{2,1,0:T(8,128)(2,1)S(1)} %get-tuple-element.20), channel_id=1, source_target_pairs={{0,2},{1,31},{2,4},{3,1},{4,6},{5,3},{6,8},{7,5},{8,10},{9,7},{10,... | collective-permute-start | bytes 786440 | tf_op jit(solution)/shard_map/ppermute | solution.py:222
  97.0 9.6 %collective-permute-start.1 = (bf16[4,256,128]{2,1,0:T(8,128)(2,1)}, bf16[4,256,128]{2,1,0:T(8,128)(2,1)S(1)}, u32[]{:S(2)}, u32[]{:S(2)}) collective-permute-start(bf16[4,256,128]{2,1,0:T(8,128)(2,1)} %get-tuple-element.19), channel_id=1, source_target_pairs={{0,30},{1,3},{2,0},{3,5},{4,2},{5,7},{6,4},{7,9},{8,6},{9,11},{10,... | collective-permute-start | bytes 786440 | tf_op jit(solution)/shard_map/ppermute | solution.py:222
  102.2 9.5 %collective-permute-start.3 = (bf16[4,256,128]{2,1,0:T(8,128)(2,1)S(1)}, bf16[4,256,128]{2,1,0:T(8,128)(2,1)S(1)}, u32[]{:S(2)}, u32[]{:S(2)}) collective-permute-start(bf16[4,256,128]{2,1,0:T(8,128)(2,1)S(1)} %fusion.2), channel_id=1, source_target_pairs={{0,2},{1,31},{2,4},{3,1},{4,6},{5,3},{6,8},{7,5},{8,10},{9,7},{10,... | collective-permute-start | bytes 786440 | tf_op jit(solution)/shard_map/ppermute | solution.py:222
  112.8 13.5 %collective-permute-start.5 = (bf16[256,128]{1,0:T(8,128)(2,1)S(1)}, bf16[256,128]{1,0:T(8,128)(2,1)S(1)}, u32[]{:S(2)}, u32[]{:S(2)}) collective-permute-start(bf16[256,128]{1,0:T(8,128)(2,1)S(1)} %get-tuple-element.22), channel_id=1, source_target_pairs={{0,8},{1,25},{2,10},{3,27},{4,12},{5,29},{6,14},{7,31},{8,16},{9,1... | collective-permute-start | bytes 196616 | tf_op jit(solution)/shard_map/ppermute | solution.py:222
  116.4 11.8 %collective-permute-start.4 = (bf16[256,128]{1,0:T(8,128)(2,1)S(1)}, bf16[256,128]{1,0:T(8,128)(2,1)S(1)}, u32[]{:S(2)}, u32[]{:S(2)}) collective-permute-start(bf16[256,128]{1,0:T(8,128)(2,1)S(1)} %get-tuple-element.21), channel_id=1, source_target_pairs={{0,24},{1,9},{2,26},{3,11},{4,28},{5,13},{6,30},{7,15},{8,0},{9,17... | collective-permute-start | bytes 196616 | tf_op jit(solution)/shard_map/ppermute | solution.py:222
  126.2 10.5 %collective-permute-start.6 = (bf16[256,128]{1,0:T(8,128)(2,1)S(1)}, bf16[256,128]{1,0:T(8,128)(2,1)S(1)}, u32[]{:S(2)}, u32[]{:S(2)}) collective-permute-start(bf16[256,128]{1,0:T(8,128)(2,1)S(1)} %fusion.6), channel_id=1, source_target_pairs={{0,8},{1,25},{2,10},{3,27},{4,12},{5,29},{6,14},{7,31},{8,16},{9,1... | collective-permute-start | bytes 196616 | tf_op jit(solution)/shard_map/ppermute | solution.py:222

commit v2 on v0

--- a/solution.py
+++ b/solution.py
@@ -18,15 +18,14 @@
     return lax.dot_general(a, b, dims, preferred_element_type=F32)
 
 
-def call(kernel, out, *args, flops=0, vmem=16, stream=False, scratch=()):
+def call(kernel, out, *args, flops=0, vmem=16):
     spec = pl.BlockSpec(memory_space=pltpu.VMEM)
     moved = sum(a.size * a.dtype.itemsize for a in args) + sum(o.size * o.dtype.itemsize for o in out)
     return pl.pallas_call(
         kernel,
         out_shape=list(out),
-        in_specs=[pl.BlockSpec(memory_space=pltpu.HBM) if stream else spec] * len(args),
+        in_specs=[spec] * len(args),
         out_specs=[spec] * len(out),
-        scratch_shapes=list(scratch),
         compiler_params=pltpu.CompilerParams(vmem_limit_bytes=vmem * 1024 * 1024),
         cost_estimate=pl.CostEstimate(flops=flops, bytes_accessed=moved, transcendentals=0),
     )(*args)
@@ -40,15 +39,10 @@
     return lax.broadcasted_iota(jnp.int32, dims, axis)
 
 
-def route_kernel(chosen_hbm, tok_hbm, up_hbm, blocks_ref, sender_ref, packer_ref, chosen_ref, tok_ref, up_ref, sem):
-    pairs = ((chosen_hbm, chosen_ref), (tok_hbm, tok_ref), (up_hbm, up_ref))
-    loads = [pltpu.make_async_copy(a, b, sem.at[i]) for i, (a, b) in enumerate(pairs)]
-    for load in loads:
-        load.start()
-    loads[0].wait()
+def route_kernel(chosen_ref, both_ref, blocks_ref, sender_ref, packer_ref):
     col = lax.axis_index("expert")
     experts, cap = chosen_ref.shape
-    count = tok_ref.shape[0]
+    count = both_ref.shape[0]
     slots = experts * SLOT
     token = iota((count, cap), 0) + col * count
     lane = iota((count, experts), 1)
@@ -63,9 +57,7 @@
     place = (iota((count, slots), 1) % SLOT).astype(F32)
     sender = jnp.logical_and(mm(mask, spread) > 0.5, mm(rank, spread) == place).astype(F32).astype(BF16)
     sender_ref[...] = sender
-    loads[1].wait()
-    loads[2].wait()
-    blocks_ref[...] = mm(sender, jnp.concatenate([tok_ref[...], up_ref[...]], axis=1), FIRST).astype(BF16)
+    blocks_ref[...] = mm(sender, both_ref[...], FIRST).astype(BF16)
     own = chosen_ref[pl.ds(col, 1), :] // count
     block = iota((slots, cap), 0) // SLOT
     held = jnp.sum((own == block).astype(F32), axis=1, keepdims=True)
@@ -176,14 +168,7 @@
     blocks, sender, packer = call(
         route_kernel,
         [shape((slots, 2 * width), BF16), shape((count, slots), BF16), shape((slots, cap), BF16)],
-        chosen, tokens, upstream,
-        stream=True,
-        scratch=[
-            pltpu.VMEM(chosen.shape, jnp.int32),
-            pltpu.VMEM(tokens.shape, BF16),
-            pltpu.VMEM(upstream.shape, BF16),
-            pltpu.SemaphoreType.DMA((3,)),
-        ],
+        chosen, jnp.concatenate([tokens, upstream], axis=1),
     )
     arrived = lax.all_to_all(blocks.reshape(experts, SLOT, 2 * width), "expert", 0, 0, tiled=True)
     (rows,) = call(pack_kernel, [shape((cap + 16, 2 * width), BF16)], arrived.reshape(slots, 2 * width), packer)

time: 149 us -> 148 us (level)
  local copies, waits for them, and re-layouts: 3.11 us -> 1.59 us
    unnamed x15 -> x11, local copies, waits for them, and re-layouts: 3.11 us -> 1.59 us
where the time goes in v2:
time: 148 us
  blocking collectives  116 us (78%)
  starting transfers between devices  13.7 us (9%)
  waiting for transfers between devices  9.59 us (6%)
  Pallas kernels  3.78 us (3%)
  other arithmetic  2.25 us (2%)
  local copies, waits for them, and re-layouts  1.59 us (1%)
    all_gather x1, blocking collectives, body(): full = lax.all_gather(rows.astype(jnp.float16), 'hidden', axis=0)  52.4 us
    all_to_all x1, blocking collectives, body(): lax.all_to_all(blocks.reshape(experts, SLOT, 2 * width), 'expert', 0, 0,...  26.8 us
    all_to_all x1, blocking collectives, body(): lax.all_to_all(near, 'hidden', 0, 0, tiled=True, axis_index_groups=groups)  22.6 us
    all_to_all x1, blocking collectives, body(): lax.all_to_all(outgoing.reshape(experts, SLOT, width), 'expert', 0, 0, ti...  14 us
    ppermute x3, starting transfers between devices, shift(): return lax.ppermute(v.astype(BF16), 'hidden', to).astype(F32)  11.4 us
    ppermute x3, waiting for transfers between devices, shift(): return lax.ppermute(v.astype(BF16), 'hidden', to).astype(F32)  7.81 us
    pallas_call x4, Pallas kernels, call(): pl.pallas_call(kernel, out_shape=list(out), in_specs=[spec] * len(args),...  3.78 us
  transfers between devices with their start and end apart: 4, of which 3 were waited for; matrix products, arithmetic and copies ran while one was open for 0% of the time, Pallas kernels for 0%

profile of v2, /device:TPU:8, one launch (start us, length us, event | category | flops | bytes accessed | tf_op | source)
XLA Modules:
  0.0 148.0 jit_solution(4310961558733147520)
XLA Ops:
  0.0 0.8 pad_maximum_fusion.both_ref
  0.8 0.0 copy-start.4
  0.8 0.8 copy-done.4
  1.5 1.2 shard_map.73
  2.7 26.8 %all_to_all.15 = bf16[32,16,256]{2,1,0:T(8,128)(2,1)S(1)} all-to-all(bf16[32,16,256]{2,1,0:T(8,128)(2,1)S(1)} %bitcast.22), channel_id=1, replica_groups=mesh['expert'=32,'hidden'=32] {'expert'}, dimensions={0} | all-to-all | bytes 524288 | tf_op jit(solution)/shard_map/all_to_all | solution.py:173
  29.5 0.4 shard_map.74
  30.0 52.4 %all-gather.2 = f16[8704,256]{1,0:T(8,128)(2,1)S(1)} all-gather(f16[272,256]{1,0:T(8,128)(2,1)S(1)} %convert_element_type.53), channel_id=2, replica_groups=mesh['expert'=32,'hidden'=32] {'hidden'}, dimensions={0}, use_global_device_ids=true | all-gather | bytes 4595712 | tf_op jit(solution)/shard_map/all_gather | solution.py:175
  82.4 0.1 fusion.10
  82.5 0.0 copy-start
  82.5 0.0 copy-start.1
  82.5 0.0 copy-start.2
  82.5 0.0 copy-start.3
  82.5 1.0 multiply_convert_fusion.x_ref
  83.6 0.1 copy-done
  83.7 0.3 copy-done.1
  84.0 0.3 copy-done.2
  84.4 0.0 copy-done.3
  84.4 1.7 %shard_map.75 = (bf16[16,256,128]{2,1,0:T(8,128)(2,1)S(1)}, bf16[256,256]{1,0:T(8,128)(2,1)S(1)}, f32[256,128]{1,0:T(8,128)S(1)}, f32[1,4096]{1,0:T(1,128)S(1)}) custom-call(bf16[32,256,256]{2,1,0:T(8,128)(2,1)S(1)} %multiply_convert_fusion.x_ref, bf16[4096,128]{1,0:T(8,128)(2,1)S(1)} %bitcast.16, bf16[4096,128]{1,0:T(8,128)(2,1)S(1)} %bitcast.18, ...), custom_call_target="tpu_custom_call" | custom-call | flops 1073741824 | bytes 8929280 | tf_op jit(solution)/shard_map/pallas_call | solution.py:24
  86.1 2.3 %collective-permute-start = (bf16[16,256,128]{2,1,0:T(8,128)(2,1)S(1)}, bf16[16,256,128]{2,1,0:T(8,128)(2,1)S(1)}, u32[]{:S(2)}, u32[]{:S(2)}) collective-permute-start(bf16[16,256,128]{2,1,0:T(8,128)(2,1)S(1)} %get-tuple-element.18), channel_id=1, source_target_pairs={{0,1},{1,0},{2,3},{3,2},{4,5},{5,4},{6,7},{7,6},{8,9},{9,8},{10,11... | collective-permute-start | bytes 3145736 | tf_op jit(solution)/shard_map/ppermute | solution.py:190
  88.4 0.5 shard_map.76
  88.9 1.8 %collective-permute-done = bf16[16,256,128]{2,1,0:T(8,128)(2,1)S(1)} collective-permute-done((bf16[16,256,128]{2,1,0:T(8,128)(2,1)S(1)}, bf16[16,256,128]{2,1,0:T(8,128)(2,1)S(1)}, u32[]{:S(2)}, u32[]{:S(2)}) %collective-permute-start) | collective-permute-done | bytes 1048608 | tf_op jit(solution)/shard_map/ppermute | solution.py:190
  90.7 0.1 fusion.3
  90.8 4.5 %collective-permute-start.2 = (bf16[4,256,128]{2,1,0:T(8,128)(2,1)S(1)}, bf16[4,256,128]{2,1,0:T(8,128)(2,1)S(1)}, u32[]{:S(2)}, u32[]{:S(2)}) collective-permute-start(bf16[4,256,128]{2,1,0:T(8,128)(2,1)S(1)} %get-tuple-element.20), channel_id=1, source_target_pairs={{0,2},{1,31},{2,4},{3,1},{4,6},{5,3},{6,8},{7,5},{8,10},{9,7},{10,... | collective-permute-start | bytes 786440 | tf_op jit(solution)/shard_map/ppermute | solution.py:207
  95.3 2.6 %collective-permute-start.1 = (bf16[4,256,128]{2,1,0:T(8,128)(2,1)S(1)}, bf16[4,256,128]{2,1,0:T(8,128)(2,1)S(1)}, u32[]{:S(2)}, u32[]{:S(2)}) collective-permute-start(bf16[4,256,128]{2,1,0:T(8,128)(2,1)S(1)} %get-tuple-element.19), channel_id=1, source_target_pairs={{0,30},{1,3},{2,0},{3,5},{4,2},{5,7},{6,4},{7,9},{8,6},{9,11},{10,... | collective-permute-start | bytes 786440 | tf_op jit(solution)/shard_map/ppermute | solution.py:207
  97.8 2.7 %collective-permute-done.2 = bf16[4,256,128]{2,1,0:T(8,128)(2,1)S(1)} collective-permute-done((bf16[4,256,128]{2,1,0:T(8,128)(2,1)S(1)}, bf16[4,256,128]{2,1,0:T(8,128)(2,1)S(1)}, u32[]{:S(2)}, u32[]{:S(2)}) %collective-permute-start.2) | collective-permute-done | bytes 262176 | tf_op jit(solution)/shard_map/ppermute | solution.py:207
  100.6 0.1 fusion.2
  100.7 4.4 %collective-permute-start.3 = (bf16[4,256,128]{2,1,0:T(8,128)(2,1)S(1)}, bf16[4,256,128]{2,1,0:T(8,128)(2,1)S(1)}, u32[]{:S(2)}, u32[]{:S(2)}) collective-permute-start(bf16[4,256,128]{2,1,0:T(8,128)(2,1)S(1)} %fusion.2), channel_id=1, source_target_pairs={{0,2},{1,31},{2,4},{3,1},{4,6},{5,3},{6,8},{7,5},{8,10},{9,7},{10,... | collective-permute-start | bytes 786440 | tf_op jit(solution)/shard_map/ppermute | solution.py:207
  105.1 0.0 collective-permute-done.1
  105.1 5.1 %collective-permute-done.3 = bf16[4,256,128]{2,1,0:T(8,128)(2,1)S(1)} collective-permute-done((bf16[4,256,128]{2,1,0:T(8,128)(2,1)S(1)}, bf16[4,256,128]{2,1,0:T(8,128)(2,1)S(1)}, u32[]{:S(2)}, u32[]{:S(2)}) %collective-permute-start.3) | collective-permute-done | bytes 262176 | tf_op jit(solution)/shard_map/ppermute | solution.py:207
  110.2 0.1 fusion.6
  110.3 22.6 %all_to_all.16 = bf16[4,256,128]{2,1,0:T(8,128)(2,1)S(1)} all-to-all(bf16[4,256,128]{2,1,0:T(8,128)(2,1)S(1)} %fusion.6), channel_id=1, replica_groups={{0,8,16,24},{1,9,17,25},{2,10,18,26},{3,11,19,27},{4,12,20,28},{5,13,21..., dimensions={0} | all-to-all | bytes 524288 | tf_op jit(solution)/shard_map/all_to_all | solution.py:212
  132.9 0.2 convolution_convert_fusion
  133.2 14.0 %all_to_all.17 = bf16[32,16,128]{2,1,0:T(8,128)(2,1)S(1)} all-to-all(bf16[32,16,128]{2,1,0:T(8,128)(2,1)S(1)} %bitcast.26), channel_id=1, replica_groups=mesh['expert'=32,'hidden'=32] {'expert'}, dimensions={0} | all-to-all | bytes 262144 | tf_op jit(solution)/shard_map/all_to_all | solution.py:215
  147.2 0.8 convolution_convert_fusion.1
  (3 shorter events, 0.1 us)
Async XLA Ops:
  0.8 0.8 copy-start.4
  82.5 1.2 copy-start
  82.5 1.5 %copy-start.1 = (bf16[1,4096,128]{2,1,0:T(8,128)(2,1)S(1)}, bf16[1,4096,128]{2,1,0:T(8,128)(2,1)}, u32[]{:S(2)}) copy-start(bf16[1,4096,128]{2,1,0:T(8,128)(2,1)} %param.11) | copy-start | bytes 3145732
  82.5 1.8 %copy-start.2 = (bf16[1,128,4096]{2,1,0:T(8,128)(2,1)S(1)}, bf16[1,128,4096]{2,1,0:T(8,128)(2,1)}, u32[]{:S(2)}) copy-start(bf16[1,128,4096]{2,1,0:T(8,128)(2,1)} %param.12) | copy-start | bytes 3145732
  82.5 1.9 %copy-start.3 = (bf16[4096,32]{0,1:T(8,128)(2,1)S(1)}, bf16[4096,32]{0,1:T(8,128)(2,1)}, u32[]{:S(2)}) copy-start(bf16[4096,32]{0,1:T(8,128)(2,1)} %param.9) | copy-start | bytes 786436
  86.1 4.6 %collective-permute-start = (bf16[16,256,128]{2,1,0:T(8,128)(2,1)S(1)}, bf16[16,256,128]{2,1,0:T(8,128)(2,1)S(1)}, u32[]{:S(2)}, u32[]{:S(2)}) collective-permute-start(bf16[16,256,128]{2,1,0:T(8,128)(2,1)S(1)} %get-tuple-element.18), channel_id=1, source_target_pairs={{0,1},{1,0},{2,3},{3,2},{4,5},{5,4},{6,7},{7,6},{8,9},{9,8},{10,11... | collective-permute-start | bytes 3145736 | tf_op jit(solution)/shard_map/ppermute | solution.py:190
  90.8 9.8 %collective-permute-start.2 = (bf16[4,256,128]{2,1,0:T(8,128)(2,1)S(1)}, bf16[4,256,128]{2,1,0:T(8,128)(2,1)S(1)}, u32[]{:S(2)}, u32[]{:S(2)}) collective-permute-start(bf16[4,256,128]{2,1,0:T(8,128)(2,1)S(1)} %get-tuple-element.20), channel_id=1, source_target_pairs={{0,2},{1,31},{2,4},{3,1},{4,6},{5,3},{6,8},{7,5},{8,10},{9,7},{10,... | collective-permute-start | bytes 786440 | tf_op jit(solution)/shard_map/ppermute | solution.py:207
  95.3 9.8 %collective-permute-start.1 = (bf16[4,256,128]{2,1,0:T(8,128)(2,1)S(1)}, bf16[4,256,128]{2,1,0:T(8,128)(2,1)S(1)}, u32[]{:S(2)}, u32[]{:S(2)}) collective-permute-start(bf16[4,256,128]{2,1,0:T(8,128)(2,1)S(1)} %get-tuple-element.19), channel_id=1, source_target_pairs={{0,30},{1,3},{2,0},{3,5},{4,2},{5,7},{6,4},{7,9},{8,6},{9,11},{10,... | collective-permute-start | bytes 786440 | tf_op jit(solution)/shard_map/ppermute | solution.py:207
  100.7 9.5 %collective-permute-start.3 = (bf16[4,256,128]{2,1,0:T(8,128)(2,1)S(1)}, bf16[4,256,128]{2,1,0:T(8,128)(2,1)S(1)}, u32[]{:S(2)}, u32[]{:S(2)}) collective-permute-start(bf16[4,256,128]{2,1,0:T(8,128)(2,1)S(1)} %fusion.2), channel_id=1, source_target_pairs={{0,2},{1,31},{2,4},{3,1},{4,6},{5,3},{6,8},{7,5},{8,10},{9,7},{10,... | collective-permute-start | bytes 786440 | tf_op jit(solution)/shard_map/ppermute | solution.py:207
